TPU v7x, 32 devices: a whole 2x2x4 slice. The times are simulated.
32 devices in a mesh: dp: 8 (over z, y), grp: 4 (over x, core).
Axes of the slice: x: 2, y: 2, z: 4, core: 2. Of those that a mesh axis runs over, the one named last changes fastest.
Arguments:
- frames: bfloat16 [96, 256, 1024], P(('dp', 'grp')), may hold values from -6 to 6
- episode_len: int32 [12], replicated, may hold values from 1 to 48, 96 in all
- norm_spatial: float32 [1024], replicated, may hold values from 0.25 to 1.75
- w_sqkv: bfloat16 [1024, 3072], replicated
- w_so: bfloat16 [1024, 1024], replicated, may hold values from -0.1875 to 0.1875
- norm_temporal: float32 [1024], replicated, may hold values from 0.25 to 1.75
- w_tqkv: bfloat16 [1024, 3072], P(('dp', 'grp'))
- w_to: bfloat16 [1024, 1024], P(('dp', 'grp')), may hold values from -0.1875 to 0.1875
Outputs:
- block_out: bfloat16 [96, 256, 1024], P(('dp', 'grp'))
Inputs may be any that keep to these rules, and one draw needn't show every extreme that they name: episode_len lists consecutive episodes that together cover all 96 frames; the longest has exactly 48 frames.
All inputs are finite; a program needn't handle non-finite values.
Results may differ from a plain program's by a relative error of at most 0.029.
The roundings to bfloat16 on the way count: a program that leaves them out, or rounds other values in their place, can miss the bound.
Values may be sent and summed in bfloat16 or wider, within the bound.
A program may use at most 128 MiB of HBM per device.

v0:
```python
import jax
import jax.numpy as jnp
from jax import lax
from jax.sharding import PartitionSpec as P

HEADS = 16


def normed(values, gain):
    wide = values.astype(jnp.float32)
    scale = lax.rsqrt(jnp.mean(wide * wide, axis=-1, keepdims=True) + 1e-06)
    return (wide * scale * gain).astype(jnp.bfloat16)


def softmax_rows(scores):
    top = jnp.max(scores, axis=-1, keepdims=True)
    weights = jnp.exp(scores - top)
    return (weights / jnp.sum(weights, axis=-1, keepdims=True)).astype(jnp.bfloat16)


def local(frames, episode_len, norm_spatial, w_sqkv, w_so, norm_temporal, w_tqkv, w_to):
    count, tokens, width = frames.shape
    head_dim = width // HEADS
    scale = head_dim ** (-0.5)
    full_tqkv, full_to = (
        lax.all_gather(w_tqkv, ("dp", "grp"), axis=0, tiled=True),
        lax.all_gather(w_to, ("dp", "grp"), axis=0, tiled=True),
    )
    hidden = normed(frames, norm_spatial).reshape(count * tokens, width)
    sqkv = jnp.dot(hidden, w_sqkv, preferred_element_type=jnp.float32).astype(jnp.bfloat16)
    sqkv = sqkv.reshape(count, tokens, 3 * width)

    def spatial_frame(block):
        queries = block[:, :width].reshape(tokens, HEADS, head_dim)
        keys_part = block[:, width : 2 * width].reshape(tokens, HEADS, head_dim)
        values_part = block[:, 2 * width :].reshape(tokens, HEADS, head_dim)
        scores = (
            jnp.einsum("phd,qhd->hpq", queries, keys_part, preferred_element_type=jnp.float32)
            * scale
        )
        probs = softmax_rows(scores)
        heads = jnp.einsum("hpq,qhd->phd", probs, values_part, preferred_element_type=jnp.float32)
        return heads.astype(jnp.bfloat16).reshape(tokens, width)

    spatial_heads = lax.map(spatial_frame, sqkv).reshape(count * tokens, width)
    update = jnp.dot(spatial_heads, w_so, preferred_element_type=jnp.float32).reshape(
        count, tokens, width
    )
    mixed = (frames.astype(jnp.float32) + update).astype(jnp.bfloat16)
    temporal_in = normed(mixed, norm_temporal)
    columns = lax.all_to_all(temporal_in, ("dp", "grp"), split_axis=1, concat_axis=0, tiled=True)
    total, local_pos, _ = columns.shape
    tqkv = jnp.dot(
        columns.reshape(total * local_pos, width), full_tqkv, preferred_element_type=jnp.float32
    )
    tqkv = tqkv.astype(jnp.bfloat16).reshape(total, local_pos, 3 * width)
    ends = jnp.cumsum(episode_len)
    position = jnp.arange(total, dtype=jnp.int32)
    episode = jnp.sum((position[:, None] >= ends[None, :]).astype(jnp.int32), axis=1)
    allowed = (position[None, :] <= position[:, None]) & (episode[None, :] == episode[:, None])
    outputs = []
    for slot_index in range(local_pos):
        block = tqkv[:, slot_index]
        queries = block[:, :width].reshape(total, HEADS, head_dim)
        keys_part = block[:, width : 2 * width].reshape(total, HEADS, head_dim)
        values_part = block[:, 2 * width :].reshape(total, HEADS, head_dim)
        scores = (
            jnp.einsum("fhd,ghd->hfg", queries, keys_part, preferred_element_type=jnp.float32)
            * scale
        )
        scores = jnp.where(allowed[None], scores, -1e30)
        probs = softmax_rows(scores)
        heads = jnp.einsum("hfg,ghd->fhd", probs, values_part, preferred_element_type=jnp.float32)
        outputs.append(heads.astype(jnp.bfloat16).reshape(total, width))
    temporal_heads = jnp.stack(outputs, axis=1).reshape(total * local_pos, width)
    temporal_update = jnp.dot(temporal_heads, full_to, preferred_element_type=jnp.float32).astype(
        jnp.bfloat16
    )
    temporal_update = temporal_update.reshape(total, local_pos, width)
    returned = lax.all_to_all(
        temporal_update, ("dp", "grp"), split_axis=0, concat_axis=1, tiled=True
    )
    return (mixed.astype(jnp.float32) + returned.astype(jnp.float32)).astype(jnp.bfloat16)


def solution(mesh):
    placed = (
        P(("dp", "grp"), None, None),
        P(),
        P(),
        P(),
        P(),
        P(),
        P(("dp", "grp"), None),
        P(("dp", "grp"), None),
    )
    return jax.shard_map(
        local, mesh=mesh, in_specs=placed, out_specs=P(("dp", "grp"), None, None), check_vma=False
    )
```

profile of v0, /device:TPU:31, one launch (start us, length us, event | category | flops | bytes accessed | tf_op | source)
XLA Modules:
  0.0 262.1 jit_solution(6698513364677343393)
XLA Ops:
  7.3 1.9 fusion.19
  9.7 9.5 %convolution_convert_fusion.1 = bf16[768,3072]{1,0:T(8,128)(2,1)} fusion(bf16[768,1024]{1,0:T(8,128)(2,1)S(1)} %bitcast.188, bf16[1024,3072]{1,0:T(8,128)(2,1)} %param.13), kind=kOutput, calls=%fused_computation.21 | convolution fusion | flops 4834197504 | bytes 12582912 | tf_op jit(solution)/shard_map/dot_general | solution.py:30
  19.2 47.1 %while.10 = (s32[]{:T(128)}, bf16[3,256,1024]{1,2,0:T(8,128)(2,1)}, bf16[3,256,3072]{2,1,0:T(8,128)(2,1)}, s32[]{:T(128)}) while((s32[]{:T(128)}, bf16[3,256,1024]{1,2,0:T(8,128)(2,1)}, bf16[3,256,3072]{2,1,0:T(8,128)(2,1)}, s32[]{:T(128)}) %tuple.65), condition=%wide.region_4.5_spmd, body=%wide.region_1.4_spmd.sunk | while | flops 273940736 | bytes 21004856 | solution.py:45
  19.2 2.8 %constant_dynamic-slice_fusion.2 = bf16[1,256,3072]{2,1,0:T(8,128)(2,1)} fusion(bf16[3,256,3072]{2,1,0:T(8,128)(2,1)} %get-tuple-element.130, s32[]{:T(128)} %get-tuple-element.124), kind=kLoop, calls=%fused_computation.10.clone.1 | loop fusion | bytes 3145732 | tf_op jit(solution)/shard_map/while/body/jit(dynamic_index_in_dim)/dynamic_slice | solution.py:45
  21.9 2.6 copy.291
  24.5 2.3 fusion.171
  26.8 4.6 %fusion.172 = (f32[16,256]{1,0:T(8,128)S(1)}, f32[16,256,256]{1,2,0:T(8,128)}) fusion(bf16[256,16,64]{0,2,1:T(8,128)(2,1)} %bitcast.184, bf16[256,16,64]{0,2,1:T(8,128)(2,1)S(1)} %bitcast.183), kind=kOutput, calls=%fused_computation.131.clone.1 | convolution fusion | flops 137363712 | bytes 5259264 | tf_op jit(solution)/shard_map/while/body/eval_jaxpr/sub | solution.py:17
  31.4 2.7 %fusion.173 = bf16[16,64,256]{2,1,0:T(8,128)(2,1)S(1)} fusion(bf16[256,16,64]{0,2,1:T(8,128)(2,1)S(1)} %bitcast.182, f32[16,256,256]{1,2,0:T(8,128)} %get-tuple-element.118, f32[16,256]{1,0:T(8,128)S(1)} %get-tuple-element.119), kind=kOutput, calls=%fused_computation.7.clone.1 | convolution fusion | flops 136577024 | bytes 5259264 | tf_op jit(solution)/shard_map/while/body/eval_jaxpr/hpq,qhd->phd/dot_general | solution.py:42
  34.9 2.7 %constant_dynamic-slice_fusion.2 = bf16[1,256,3072]{2,1,0:T(8,128)(2,1)} fusion(bf16[3,256,3072]{2,1,0:T(8,128)(2,1)} %get-tuple-element.130, s32[]{:T(128)} %get-tuple-element.124), kind=kLoop, calls=%fused_computation.10.clone.1 | loop fusion | bytes 3145732 | tf_op jit(solution)/shard_map/while/body/jit(dynamic_index_in_dim)/dynamic_slice | solution.py:45
  37.6 2.6 copy.291
  40.2 2.3 fusion.171
  42.4 4.6 %fusion.172 = (f32[16,256]{1,0:T(8,128)S(1)}, f32[16,256,256]{1,2,0:T(8,128)}) fusion(bf16[256,16,64]{0,2,1:T(8,128)(2,1)} %bitcast.184, bf16[256,16,64]{0,2,1:T(8,128)(2,1)S(1)} %bitcast.183), kind=kOutput, calls=%fused_computation.131.clone.1 | convolution fusion | flops 137363712 | bytes 5259264 | tf_op jit(solution)/shard_map/while/body/eval_jaxpr/sub | solution.py:17
  47.0 2.7 %fusion.173 = bf16[16,64,256]{2,1,0:T(8,128)(2,1)S(1)} fusion(bf16[256,16,64]{0,2,1:T(8,128)(2,1)S(1)} %bitcast.182, f32[16,256,256]{1,2,0:T(8,128)} %get-tuple-element.118, f32[16,256]{1,0:T(8,128)S(1)} %get-tuple-element.119), kind=kOutput, calls=%fused_computation.7.clone.1 | convolution fusion | flops 136577024 | bytes 5259264 | tf_op jit(solution)/shard_map/while/body/eval_jaxpr/hpq,qhd->phd/dot_general | solution.py:42
  50.6 2.7 %constant_dynamic-slice_fusion.2 = bf16[1,256,3072]{2,1,0:T(8,128)(2,1)} fusion(bf16[3,256,3072]{2,1,0:T(8,128)(2,1)} %get-tuple-element.130, s32[]{:T(128)} %get-tuple-element.124), kind=kLoop, calls=%fused_computation.10.clone.1 | loop fusion | bytes 3145732 | tf_op jit(solution)/shard_map/while/body/jit(dynamic_index_in_dim)/dynamic_slice | solution.py:45
  53.3 2.6 copy.291
  55.8 2.3 fusion.171
  58.1 4.6 %fusion.172 = (f32[16,256]{1,0:T(8,128)S(1)}, f32[16,256,256]{1,2,0:T(8,128)}) fusion(bf16[256,16,64]{0,2,1:T(8,128)(2,1)} %bitcast.184, bf16[256,16,64]{0,2,1:T(8,128)(2,1)S(1)} %bitcast.183), kind=kOutput, calls=%fused_computation.131.clone.1 | convolution fusion | flops 137363712 | bytes 5259264 | tf_op jit(solution)/shard_map/while/body/eval_jaxpr/sub | solution.py:17
  62.7 2.7 %fusion.173 = bf16[16,64,256]{2,1,0:T(8,128)(2,1)S(1)} fusion(bf16[256,16,64]{0,2,1:T(8,128)(2,1)S(1)} %bitcast.182, f32[16,256,256]{1,2,0:T(8,128)} %get-tuple-element.118, f32[16,256]{1,0:T(8,128)S(1)} %get-tuple-element.119), kind=kOutput, calls=%fused_computation.7.clone.1 | convolution fusion | flops 136577024 | bytes 5259264 | tf_op jit(solution)/shard_map/while/body/eval_jaxpr/hpq,qhd->phd/dot_general | solution.py:42
  66.3 4.0 %fusion.23 = (f32[3,256]{1,0:T(4,128)S(1)}, bf16[3,256,1024]{2,1,0:T(8,128)(2,1)S(1)}) fusion(bf16[3,256,1024]{1,2,0:T(8,128)(2,1)} %get-tuple-element.22, bf16[1024,1024]{1,0:T(8,128)(2,1)S(1)} %copy-done, bf16[3,256,1024]{2,1,0:T(8,128)(2,1)} %param.10), kind=kOutput, calls=%fused_computation.33 | convolution fusion | flops 1615330560 | bytes 6818816 | tf_op jit(solution)/shard_map/dot_general | solution.py:46
  70.3 1.1 copy-done.3
  71.9 2.7 %copy.208 = bf16[3,256,1024]{2,0,1:T(4,128)(2,1)} copy(bf16[3,256,1024]{2,1,0:T(8,128)(2,1)S(1)} %fusion.25) | data formatting | bytes 3145728 | tf_op jit(solution)/shard_map/convert_element_type | solution.py:12
  74.6 6.4 %all-to-all-start = ((bf16[3,256,1024]{2,0,1:T(4,128)(2,1)}), bf16[3,256,1024]{2,0,1:T(4,128)(2,1)S(1)}, u32[]{:S(2)}, u32[]{:S(2)}) async-start(bf16[3,256,1024]{2,0,1:T(4,128)(2,1)} %copy.208), calls=%async_computation | async-start | bytes 4194304 | tf_op jit(solution)/shard_map/all_to_all | solution.py:51
  82.2 50.0 %all-to-all-done = bf16[3,256,1024]{2,0,1:T(4,128)(2,1)S(1)} async-done(((bf16[3,256,1024]{2,0,1:T(4,128)(2,1)}), bf16[3,256,1024]{2,0,1:T(4,128)(2,1)S(1)}, u32[]{:S(2)}, u32[]{:S(2)}) %all-to-all-start) | async-done | bytes 1572896 | tf_op jit(solution)/shard_map/all_to_all | solution.py:51
  133.0 8.5 %fusion.18 = bf16[96,8,3072]{2,1,0:T(8,128)(2,1)S(1)} fusion(bf16[768,1024]{1,0:T(8,128)(2,1)S(1)} %bitcast.187, bf16[1024,3072]{1,0:T(8,128)(2,1)} %all-gather.3.cloned.1.call-done), kind=kOutput, calls=%fused_computation.28 | convolution fusion | flops 4834197504 | bytes 12582912 | tf_op jit(solution)/shard_map/dot_general | solution.py:53
  141.5 8.3 %fusion.86 = (bf16[96,1,3072]{2,1,0:T(2,128)(2,1)S(1)}, bf16[96,1,3072]{2,1,0:T(2,128)(2,1)S(1)}, bf16[96,1,3072]{2,1,0:T(2,128)(2,1)}, bf16[96,1,3072]{2,1,0:T(...) fusion(bf16[96,8,3072]{2,1,0:T(8,128)(2,1)S(1)} %fusion.18), kind=kLoop, calls=%fused_computation.132 | loop fusion | bytes 9437184 | tf_op jit(solution)/shard_map/slice | solution.py:63
  151.2 1.1 copy.249
  152.3 1.3 fusion.51
  155.1 1.2 fusion.52
  156.7 2.0 copy_bitcast_fusion.3
  159.7 1.1 copy.239
  160.8 1.2 fusion.53
  164.5 1.2 fusion.54
  166.3 1.8 convolution_convert_fusion.3
  169.4 1.7 convolution_convert_fusion.4
  172.3 1.7 convolution_convert_fusion.5
  175.3 1.7 convolution_convert_fusion.6
  178.0 2.0 copy_bitcast_fusion.5
  182.1 1.8 copy.227
  184.3 1.2 fusion.55
  185.5 1.8 convolution_convert_fusion.7
  191.0 1.2 fusion.56
  192.2 1.7 convolution_convert_fusion.8
  198.4 1.2 fusion.58
  199.7 1.8 convolution_convert_fusion.10
  202.0 6.6 %stack.3 = bf16[96,8,1024]{2,1,0:T(8,128)(2,1)} concatenate(bf16[96,1,1024]{2,1,0:T(2,128)(2,1)S(1)} %copy.251, bf16[96,1,1024]{2,1,0:T(2,128)(2,1)S(1)} %copy.252, bf16[96,1,1024]{2,1,0:T(2,128)(2,1)S(1)} %copy-done.10, bf16[96,1,1024]{2,1,0:T(2,128)(2,1)S(1)} %copy-done.9, bf16[96,1,1024]{2,1,0:T(2,128)(2,1)S(1)} %copy-done.8, bf16[96,1,1024]{2,1,0:T(2,128)(2,1)S(1)} %copy-done.7, ...), dimensions={1} | concatenate | bytes 3145728 | tf_op jit(solution)/shard_map/stack | solution.py:75
  208.6 3.9 %fusion.32 = bf16[96,8,1024]{2,1,0:T(8,128)(2,1)S(1)} fusion(bf16[1024,1024]{1,0:T(8,128)(2,1)} %all-gather.5.cloned.1.call-done, bf16[96,8,1024]{2,1,0:T(8,128)(2,1)} %stack.3), kind=kOutput, calls=%fused_computation.43 | convolution fusion | flops 1611399168 | bytes 5242880 | tf_op jit(solution)/shard_map/dot_general | solution.py:76
  212.5 40.9 %all_to_all.24 = bf16[96,8,1024]{2,1,0:T(8,128)(2,1)S(1)} all-to-all(bf16[96,8,1024]{2,1,0:T(8,128)(2,1)S(1)} %fusion.32), channel_id=1, replica_groups=mesh['dp'=8,'grp'=4] {'dp','grp'}, dimensions={0} | all-to-all | bytes 3145728 | tf_op jit(solution)/shard_map/all_to_all | solution.py:80
  253.4 1.8 fusion.26
  (101 shorter events, 29.3 us)
Async XLA Ops:
  6.5 59.7 %copy-start = (bf16[1024,1024]{1,0:T(8,128)(2,1)S(1)}, bf16[1024,1024]{1,0:T(8,128)(2,1)}, u32[]{:S(2)}) copy-start(bf16[1024,1024]{1,0:T(8,128)(2,1)} %param.14) | copy-start | bytes 6291460
  6.5 2.7 %copy-start.14 = (f32[1024]{0:T(1024)S(1)}, f32[1024]{0:T(1024)}, u32[]{:S(2)}) copy-start(f32[1024]{0:T(1024)} %param.12) | copy-start | bytes 12292
  6.5 126.4 %all-gather.3.cloned.1.call-start = ((), (), s32[]{:S(2)}) async-start(), calls=%async_computation.2 | async-start | bytes 6488064 | tf_op jit(solution)/shard_map/all_gather | solution.py:26
  7.3 1.9 copy-start.2
  66.3 5.2 %copy-start.15 = (f32[1024]{0:T(1024)S(1)}, f32[1024]{0:T(1024)}, u32[]{:S(2)}) copy-start(f32[1024]{0:T(1024)} %param.15) | copy-start | bytes 12292
  70.3 1.1 copy-start.3
  74.6 7.2 %copy-start.16 = (s32[12]{0:T(128)S(1)}, s32[12]{0:T(128)}, u32[]{:S(2)}) copy-start(s32[12]{0:T(128)} %param.11) | copy-start | bytes 148
  74.6 57.6 %all-to-all-start = ((bf16[3,256,1024]{2,0,1:T(4,128)(2,1)}), bf16[3,256,1024]{2,0,1:T(4,128)(2,1)S(1)}, u32[]{:S(2)}, u32[]{:S(2)}) async-start(bf16[3,256,1024]{2,0,1:T(4,128)(2,1)} %copy.208), calls=%async_computation | async-start | bytes 4194304 | tf_op jit(solution)/shard_map/all_to_all | solution.py:51
  81.1 127.5 %all-gather.5.cloned.1.call-start = ((), (), s32[]{:S(2)}) async-start(), calls=%async_computation.3 | async-start | bytes 2162688 | tf_op jit(solution)/shard_map/all_gather | solution.py:27
  164.5 1.7 copy-start.11
  166.3 2.9 %copy-start.12 = (bf16[96,1024]{1,0:T(8,128)(2,1)S(1)}, bf16[96,1024]{1,0:T(8,128)(2,1)}, u32[]{:S(2)}) copy-start(bf16[96,1024]{1,0:T(8,128)(2,1)} %get-tuple-element.62) | copy-start | bytes 589828
  169.4 2.8 %copy-start.13 = (bf16[96,1024]{1,0:T(8,128)(2,1)S(1)}, bf16[96,1024]{1,0:T(8,128)(2,1)}, u32[]{:S(2)}) copy-start(bf16[96,1024]{1,0:T(8,128)(2,1)} %get-tuple-element.65) | copy-start | bytes 589828
  199.6 2.3 copy-start.5
  199.6 2.3 copy-start.6
  199.6 2.3 copy-start.7
  199.6 2.3 copy-start.8
  199.6 2.4 copy-start.9
  199.6 2.4 copy-start.10
  212.5 40.9 %copy-start.4 = (bf16[3,256,1024]{2,1,0:T(8,128)(2,1)S(1)}, bf16[3,256,1024]{2,1,0:T(8,128)(2,1)}, u32[]{:S(2)}) copy-start(bf16[3,256,1024]{2,1,0:T(8,128)(2,1)} %copy-done.3) | copy-start | bytes 4718596
  253.4 1.9 copy-start.1
Sparse Core Ops, SparseCore 0:
  10.2 68.4 all-gather.2
  84.8 62.4 all-gather.4
where the time goes:
time: 267 us; the launch traced here: 262 us
  matrix products  72.6 us (27%)
  local copies, waits for them, and re-layouts  71.8 us (27%)
  waiting for transfers between devices  51.4 us (19%)
  blocking collectives  40.9 us (15%)
  between operations  13.9 us (5%)
  starting transfers between devices  6.49 us (2%)
  other arithmetic  4.98 us (2%)
    all_to_all x1, waiting for transfers between devices, local(): lax.all_to_all(temporal_in, ('dp', 'grp'), split_axis=1, concat_axis=0, t...  50 us
    all_to_all x1, blocking collectives, local(): lax.all_to_all(temporal_update, ('dp', 'grp'), split_axis=0, concat_axis=...  40.9 us
    sub x11, matrix products, softmax_rows(): weights = jnp.exp(scores - top)  17.5 us
    dynamic_slice x6, local copies, waits for them, and re-layouts, local(): spatial_heads = lax.map(spatial_frame, sqkv).reshape(count * tokens, width)  15.9 us
    another operation x9, local copies, waits for them, and re-layouts, local(): jnp.stack(outputs, axis=1).reshape(total * local_pos, width)  13.9 us
    dot_general x8, matrix products, local(): jnp.einsum('hfg,ghd->fhd', probs, values_part, preferred_element_type=jnp...  12.5 us
    dot_general x1, matrix products, local(): jnp.dot(hidden, w_sqkv, preferred_element_type=jnp.float32)  9.5 us
    slice x16, local copies, waits for them, and re-layouts, local(): keys_part = block[:, width:2 * width].reshape(total, HEADS, head_dim)  8.84 us
  transfers between devices with their start and end apart: 3, of which 1 were waited for; matrix products, arithmetic and copies ran while one was open for 54% of the time, Pallas kernels for 0%

commit v1 on v0

--- a/solution.py
+++ b/solution.py
@@ -1,21 +1,173 @@
+import functools
+
 import jax
 import jax.numpy as jnp
 from jax import lax
+from jax.experimental import pallas as pl
+from jax.experimental.pallas import tpu as pltpu
 from jax.sharding import PartitionSpec as P
 
 HEADS = 16
+F32 = jnp.float32
+BF16 = jnp.bfloat16
+NT = (((1,), (1,)), ((), ()))
 
 
 def normed(values, gain):
-    wide = values.astype(jnp.float32)
+    wide = values.astype(F32)
     scale = lax.rsqrt(jnp.mean(wide * wide, axis=-1, keepdims=True) + 1e-06)
-    return (wide * scale * gain).astype(jnp.bfloat16)
+    return (wide * scale * gain).astype(BF16)
 
 
 def softmax_rows(scores):
     top = jnp.max(scores, axis=-1, keepdims=True)
     weights = jnp.exp(scores - top)
-    return (weights / jnp.sum(weights, axis=-1, keepdims=True)).astype(jnp.bfloat16)
+    return (weights * (1.0 / jnp.sum(weights, axis=-1, keepdims=True))).astype(BF16)
+
+
+def pair_heads(q2, k2, v2, bias, low):
+    rows = q2.shape[0]
+    q2 = q2 * jnp.asarray(0.125, BF16)
+    zero = jnp.zeros_like(q2)
+    both = jnp.concatenate([jnp.where(low, q2, zero), jnp.where(low, zero, q2)], axis=0)
+    scores = lax.dot_general(both, k2, NT, preferred_element_type=F32)
+    if bias is not None:
+        scores = jnp.where(bias, scores, -1e30)
+    probs = softmax_rows(scores)
+    out = jnp.dot(probs, v2, preferred_element_type=F32)
+    return jnp.where(low, out[:rows], out[rows:]).astype(BF16)
+
+
+def spatial_kernel(frames, gain_s, w_qkv, w_o, gain_t, mixed, hidden_t, hidden, qkv, heads):
+    count, tokens, width = frames.shape
+    low = lax.broadcasted_iota(jnp.int32, (tokens, 128), 1) < 64
+
+    @pl.loop(0, count)
+    def _(i):
+        rows = pl.ds(pl.multiple_of(i * tokens, tokens), tokens)
+        hidden[rows, :] = normed(frames[i], gain_s[...])
+
+    @pl.loop(0, 3 * width // 256)
+    def _(t):
+        cols = pl.ds(pl.multiple_of(t * 256, 256), 256)
+        qkv[:, cols] = jnp.dot(hidden[...], w_qkv[:, cols], preferred_element_type=F32).astype(BF16)
+
+    @pl.loop(0, count)
+    def _(i):
+        rows = pl.ds(pl.multiple_of(i * tokens, tokens), tokens)
+
+        @pl.loop(0, width // 512)
+        def _(g):
+            for s in range(4):
+                c = pl.multiple_of(g * 512 + s * 128, 128)
+                heads[:, pl.ds(c, 128)] = pair_heads(
+                    qkv[rows, pl.ds(c, 128)],
+                    qkv[rows, pl.ds(c + width, 128)],
+                    qkv[rows, pl.ds(c + 2 * width, 128)],
+                    None,
+                    low,
+                )
+
+        update = jnp.dot(heads[...], w_o[...], preferred_element_type=F32)
+        block = (frames[i].astype(F32) + update).astype(BF16)
+        mixed[i] = block
+        hidden_t[i] = normed(block, gain_t[...])
+
+
+def temporal_kernel(columns, allowed, w_qkv, w_o, out, wide, hidden, qkv, heads):
+    total, local_pos, width = columns.shape
+    lanes = range(0, width, 128)
+    for g in range(0, total, 16):
+        block = columns[pl.ds(g, 16)].astype(F32).reshape(16 * local_pos, width)
+        for c in lanes:
+            wide[c // 128, pl.ds(g * local_pos, 16 * local_pos), :] = block[:, c : c + 128]
+    for p in range(local_pos):
+        for c in lanes:
+            hidden[pl.ds(p * total, total), pl.ds(c, 128)] = wide[
+                c // 128, pl.ds(p, total, stride=local_pos), :
+            ].astype(BF16)
+
+    @pl.loop(0, 3 * width // 256)
+    def _(t):
+        cols = pl.ds(pl.multiple_of(t * 256, 256), 256)
+        qkv[:, cols] = jnp.dot(hidden[...], w_qkv[:, cols], preferred_element_type=F32).astype(BF16)
+
+    mask = jnp.concatenate([allowed[...], allowed[...]], axis=0) > 0.0
+    low = lax.broadcasted_iota(jnp.int32, (total, 128), 1) < 64
+
+    @pl.loop(0, local_pos)
+    def _(p):
+        rows = pl.ds(pl.multiple_of(p * total, total), total)
+        for c in range(0, width, 128):
+            heads[rows, pl.ds(c, 128)] = pair_heads(
+                qkv[rows, pl.ds(c, 128)],
+                qkv[rows, pl.ds(c + width, 128)],
+                qkv[rows, pl.ds(c + 2 * width, 128)],
+                mask,
+                low,
+            )
+
+    for t in range(0, width, 256):
+        update = jnp.dot(heads[...], w_o[:, pl.ds(t, 256)], preferred_element_type=F32)
+        for p in range(local_pos):
+            for c in range(0, 256, 128):
+                wide[(t + c) // 128, pl.ds(p, total, stride=local_pos), :] = update[
+                    p * total : (p + 1) * total, c : c + 128
+                ]
+    for g in range(0, total, 16):
+        for c in lanes:
+            block = wide[c // 128, pl.ds(g * local_pos, 16 * local_pos), :]
+            out[pl.ds(g, 16), :, pl.ds(c, 128)] = block.reshape(16, local_pos, 128).astype(BF16)
+
+
+def allowed_frames(episode_len, total):
+    ends = jnp.cumsum(episode_len)
+    position = jnp.arange(total, dtype=jnp.int32)
+    episode = jnp.sum((position[:, None] >= ends[None, :]).astype(jnp.int32), axis=1)
+    return (position[None, :] <= position[:, None]) & (episode[None, :] == episode[:, None])
+
+
+VMEM = pl.BlockSpec(memory_space=pltpu.VMEM)
+
+
+def fused(frames, episode_len, norm_spatial, w_sqkv, w_so, norm_temporal, w_tqkv, w_to):
+    count, tokens, width = frames.shape
+    full_tqkv = lax.all_gather(w_tqkv, ("dp", "grp"), axis=0, tiled=True)
+    full_to = lax.all_gather(w_to, ("dp", "grp"), axis=0, tiled=True)
+    rows = count * tokens
+    mixed, temporal_in = pl.pallas_call(
+        spatial_kernel,
+        out_shape=[jax.ShapeDtypeStruct(frames.shape, BF16)] * 2,
+        in_specs=[VMEM] * 5,
+        out_specs=[VMEM] * 2,
+        scratch_shapes=[
+            pltpu.VMEM((rows, width), BF16),
+            pltpu.VMEM((rows, 3 * width), BF16),
+            pltpu.VMEM((tokens, width), BF16),
+        ],
+        compiler_params=pltpu.CompilerParams(vmem_limit_bytes=48 << 20),
+        name="spatial",
+    )(frames, norm_spatial.reshape(1, width), w_sqkv, w_so, norm_temporal.reshape(1, width))
+    columns = lax.all_to_all(temporal_in, ("dp", "grp"), split_axis=1, concat_axis=0, tiled=True)
+    total, local_pos, _ = columns.shape
+    allowed = allowed_frames(episode_len, total).astype(F32)
+    rows = total * local_pos
+    update = pl.pallas_call(
+        temporal_kernel,
+        out_shape=jax.ShapeDtypeStruct(columns.shape, BF16),
+        in_specs=[VMEM] * 4,
+        out_specs=VMEM,
+        scratch_shapes=[
+            pltpu.VMEM((width // 128, rows, 128), F32),
+            pltpu.VMEM((rows, width), BF16),
+            pltpu.VMEM((rows, 3 * width), BF16),
+            pltpu.VMEM((rows, width), BF16),
+        ],
+        compiler_params=pltpu.CompilerParams(vmem_limit_bytes=48 << 20),
+        name="temporal",
+    )(columns, allowed, full_tqkv, full_to)
+    returned = lax.all_to_all(update, ("dp", "grp"), split_axis=0, concat_axis=1, tiled=True)
+    return (mixed.astype(F32) + returned.astype(F32)).astype(BF16)
 
 
 def local(frames, episode_len, norm_spatial, w_sqkv, w_so, norm_temporal, w_tqkv, w_to):
@@ -94,6 +246,8 @@
         P(("dp", "grp"), None),
         P(("dp", "grp"), None),
     )
+    devices = mesh.shape["dp"] * mesh.shape["grp"]
+    body = fused if devices == 32 else local
     return jax.shard_map(
-        local, mesh=mesh, in_specs=placed, out_specs=P(("dp", "grp"), None, None), check_vma=False
-    )
+        body, mesh=mesh, in_specs=placed, out_specs=P(("dp", "grp"), None, None), check_vma=False
+    )

time: 267 us -> 223 us (0.84)
  matrix products: 72.6 us -> 0 us
  local copies, waits for them, and re-layouts: 71.8 us -> 9.39 us
  waiting for transfers between devices: 51.4 us -> 102 us
  Pallas kernels: 0 us -> 44.1 us
  other arithmetic: 4.98 us -> 2.17 us
    dot_general x23 -> x0, matrix products: 55.1 us -> none  [the longest x8 12.5 us: local(): jnp.einsum('hfg,ghd->fhd', probs, values_part, preferred_element_type=jnp...]
    pallas_call x0 -> x2, Pallas kernels: none -> 44.1 us  [the longest x1 22.6 us: fused(): pl.pallas_call(spatial_kernel, out_shape=[jax.ShapeDtypeStruct(frames.sha...]
    all_gather x2, waiting for transfers between devices: 0.02 us -> 43.6 us  [the longest x1 43.6 us: fused(): full_tqkv = lax.all_gather(w_tqkv, ('dp', 'grp'), axis=0, tiled=True)]
    slice x36 -> x0, local copies, waits for them, and re-layouts: 30.1 us -> none  [the longest x16 8.84 us: local(): keys_part = block[:, width:2 * width].reshape(total, HEADS, head_dim)]
    sub x11 -> x0, matrix products: 17.5 us -> none  [softmax_rows(): weights = jnp.exp(scores - top)]
    dynamic_slice x6 -> x0, local copies, waits for them, and re-layouts: 15.9 us -> none  [local(): spatial_heads = lax.map(spatial_frame, sqkv).reshape(count * tokens, width)]
    another operation x9 -> x0, local copies, waits for them, and re-layouts: 13.9 us -> none  [local(): jnp.stack(outputs, axis=1).reshape(total * local_pos, width)]
    all_to_all x1, waiting for transfers between devices: 50 us -> 57.1 us  [fused(): lax.all_to_all(temporal_in, ('dp', 'grp'), split_axis=1, concat_axis=0, t...]
  transfers between devices with their start and end apart: 3 -> 3, of which waited for: 1 -> 2; matrix products, arithmetic and copies ran while one was open for 54% -> 2% of each run, Pallas kernels for 0% -> 10%
where the time goes in v1:
time: 223 us; the launch traced here: 218 us
  waiting for transfers between devices  102 us (46%)
  Pallas kernels  44.1 us (20%)
  blocking collectives  40.7 us (18%)
  between operations  13.5 us (6%)
  local copies, waits for them, and re-layouts  9.39 us (4%)
  starting transfers between devices  6.24 us (3%)
    all_to_all x1, waiting for transfers between devices, fused(): lax.all_to_all(temporal_in, ('dp', 'grp'), split_axis=1, concat_axis=0, t...  57.1 us
    all_gather x1, waiting for transfers between devices, fused(): full_tqkv = lax.all_gather(w_tqkv, ('dp', 'grp'), axis=0, tiled=True)  43.6 us
    all_to_all x1, blocking collectives, fused(): lax.all_to_all(update, ('dp', 'grp'), split_axis=0, concat_axis=1, tiled=...  40.7 us
    pallas_call x1, Pallas kernels, fused(): pl.pallas_call(spatial_kernel, out_shape=[jax.ShapeDtypeStruct(frames.sha...  22.6 us
    pallas_call x1, Pallas kernels, fused(): pl.pallas_call(temporal_kernel, out_shape=jax.ShapeDtypeStruct(columns.sh...  21.5 us
    all_to_all x1, starting transfers between devices, fused(): lax.all_to_all(temporal_in, ('dp', 'grp'), split_axis=1, concat_axis=0, t...  6.2 us
  transfers between devices with their start and end apart: 3, of which 2 were waited for; matrix products, arithmetic and copies ran while one was open for 2% of the time, Pallas kernels for 10%

profile of v1, /device:TPU:31, one launch (start us, length us, event | category | flops | bytes accessed | tf_op | source)
XLA Modules:
  0.0 218.2 jit_solution(13168044850507004230)
XLA Ops:
  6.5 0.0 all-gather.5.cloned.1.call-start
  6.5 0.7 all-gather.5.cloned.1.call-update
  7.3 0.0 all-gather.3.cloned.1.call-start
  7.3 0.7 all-gather.3.cloned.1.call-update
  8.0 0.0 copy-start.1
  8.0 1.4 copy-done.1
  9.4 0.0 copy-start.2
  9.4 0.7 copy-done.2
  10.1 0.0 copy-start.3
  10.1 0.7 copy-done.3
  10.8 22.6 %spatial.1 = (bf16[3,256,1024]{2,1,0:T(8,128)(2,1)S(1)}, bf16[3,256,1024]{2,1,0:T(8,128)(2,1)S(1)}) custom-call(bf16[3,256,1024]{2,1,0:T(8,128)(2,1)S(1)} %copy-done.1, f32[1,1024]{1,0:T(1,128)S(1)} %bitcast.18, bf16[1024,3072]{1,0:T(8,128)(2,1)} %w_qkv.1, bf16[1024,1024]{1,0:T(8,128)(2,1)} %w_o.1, f32[1,1024]{1,0:T(1,128)S(1)} %bitcast.19), custom_call_target="tpu_custom_call" | custom-call | tf_op jit(solution)/shard_map/spatial/pallas_call | solution.py:138
  33.4 2.7 %copy.14 = bf16[3,256,1024]{2,0,1:T(4,128)(2,1)} copy(bf16[3,256,1024]{2,1,0:T(8,128)(2,1)S(1)} %get-tuple-element.8) | data formatting | bytes 3145728 | tf_op jit(solution)/shard_map/spatial/pallas_call | solution.py:138
  36.1 0.0 copy-start.4
  36.1 6.2 %all-to-all-start = ((bf16[3,256,1024]{2,0,1:T(4,128)(2,1)}), bf16[3,256,1024]{2,0,1:T(4,128)(2,1)}, u32[]{:S(2)}, u32[]{:S(2)}) async-start(bf16[3,256,1024]{2,0,1:T(4,128)(2,1)} %copy.14), calls=%async_computation | async-start | bytes 4194304 | tf_op jit(solution)/shard_map/all_to_all | solution.py:151
  42.3 0.0 copy-done.4
  42.3 0.2 reduce-window.8
  42.5 0.1 convert_reduce_fusion
  42.6 0.1 fusion.2.allowed
  42.7 57.1 %all-to-all-done = bf16[3,256,1024]{2,0,1:T(4,128)(2,1)} async-done(((bf16[3,256,1024]{2,0,1:T(4,128)(2,1)}), bf16[3,256,1024]{2,0,1:T(4,128)(2,1)}, u32[]{:S(2)}, u32[]{:S(2)}) %all-to-all-start) | async-done | bytes 1572896 | tf_op jit(solution)/shard_map/all_to_all | solution.py:151
  99.8 2.3 %copy.15 = bf16[3,32,8,1024]{3,2,0,1:T(8,128)(2,1)S(1)} copy(bf16[3,32,8,1024]{3,0,2,1:T(4,128)(2,1)} %bitcast.2) | data formatting | bytes 3145728 | tf_op jit(solution)/shard_map/all_to_all | solution.py:151
  102.2 0.0 all-gather.5.cloned.1.call-done.w_o
  102.2 43.6 %all-gather.3.cloned.1.call-done.w_qkv = bf16[1024,3072]{1,0:T(8,128)(2,1)} async-done(((bf16[32,3072]{1,0:T(8,128)(2,1)}), bf16[1024,3072]{1,0:T(8,128)(2,1)}) %all-gather.3.cloned.1.call-update) | async-done | bytes 6291472 | tf_op jit(solution)/shard_map/all_gather | solution.py:135
  145.8 0.0 copy-start
  145.8 1.6 copy-done
  147.4 21.5 %temporal.1 = bf16[96,8,1024]{2,1,0:T(8,128)(2,1)S(1)} custom-call(bf16[96,8,1024]{2,1,0:T(8,128)(2,1)S(1)} %bitcast.17, f32[96,96]{1,0:T(8,128)S(1)} %fusion.2.allowed, bf16[1024,3072]{1,0:T(8,128)(2,1)} %all-gather.3.cloned.1.call-done.w_qkv, bf16[1024,1024]{1,0:T(8,128)(2,1)S(1)} %copy-done), custom_call_target="tpu_custom_call" | custom-call | tf_op jit(solution)/shard_map/temporal/pallas_call | solution.py:155
  168.9 40.7 %all_to_all.27 = bf16[96,8,1024]{2,1,0:T(8,128)(2,1)S(1)} all-to-all(bf16[96,8,1024]{2,1,0:T(8,128)(2,1)S(1)} %temporal.1), channel_id=1, replica_groups=mesh['dp'=8,'grp'=4] {'dp','grp'}, dimensions={0} | all-to-all | bytes 3145728 | tf_op jit(solution)/shard_map/all_to_all | solution.py:169
  209.6 1.8 fusion
Async XLA Ops:
  6.5 95.6 %all-gather.5.cloned.1.call-start = ((), (), s32[]{:S(2)}) async-start(), calls=%async_computation.3 | async-start | bytes 2162688 | tf_op jit(solution)/shard_map/all_gather | solution.py:136
  7.3 138.5 %all-gather.3.cloned.1.call-start = ((), (), s32[]{:S(2)}) async-start(), calls=%async_computation.2 | async-start | bytes 6488064 | tf_op jit(solution)/shard_map/all_gather | solution.py:135
  8.0 1.4 copy-start.1
  9.4 0.7 copy-start.2
  10.1 0.7 copy-start.3
  36.1 6.2 %copy-start.4 = (s32[12]{0:T(128)S(1)}, s32[12]{0:T(128)}, u32[]{:S(2)}) copy-start(s32[12]{0:T(128)} %param.9) | copy-start | bytes 148
  36.1 63.7 %all-to-all-start = ((bf16[3,256,1024]{2,0,1:T(4,128)(2,1)}), bf16[3,256,1024]{2,0,1:T(4,128)(2,1)}, u32[]{:S(2)}, u32[]{:S(2)}) async-start(bf16[3,256,1024]{2,0,1:T(4,128)(2,1)} %copy.14), calls=%async_computation | async-start | bytes 4194304 | tf_op jit(solution)/shard_map/all_to_all | solution.py:151
  145.8 1.6 copy-start
Sparse Core Ops, SparseCore 0:
  10.2 62.1 all-gather.4
  75.3 70.4 all-gather.2

commit v2 on v1

--- a/solution.py
+++ b/solution.py
@@ -38,8 +38,32 @@
     return jnp.where(low, out[:rows], out[rows:]).astype(BF16)
 
 
-def spatial_kernel(frames, gain_s, w_qkv, w_o, gain_t, mixed, hidden_t, hidden, qkv, heads):
+MESH_ID = pl.DeviceIdType.MESH
+
+
+def place(index, groups):
+    return (index // groups, lax.rem(index, groups))
+
+
+def greet_all(me, devices, groups):
+    barrier = pltpu.get_barrier_semaphore()
+
+    @pl.loop(1, devices)
+    def _(k):
+        peer = lax.rem(me + k, devices)
+        pl.semaphore_signal(barrier, inc=1, device_id=place(peer, groups), device_id_type=MESH_ID)
+
+    return barrier
+
+
+def spatial_kernel(
+    groups, frames, gain_s, w_qkv, w_o, gain_t, mixed, arrived, hidden, qkv, heads, parcels,
+    send_sem, recv_sem, own_sem,
+):
     count, tokens, width = frames.shape
+    devices, half = parcels.shape[1], width // 2
+    me = lax.axis_index("dp") * groups + lax.axis_index("grp")
+    barrier = greet_all(me, devices, groups)
     low = lax.broadcasted_iota(jnp.int32, (tokens, 128), 1) < 64
 
     @pl.loop(0, count)
@@ -51,6 +75,8 @@
     def _(t):
         cols = pl.ds(pl.multiple_of(t * 256, 256), 256)
         qkv[:, cols] = jnp.dot(hidden[...], w_qkv[:, cols], preferred_element_type=F32).astype(BF16)
+
+    pl.semaphore_wait(barrier, devices - 1)
 
     @pl.loop(0, count)
     def _(i):
@@ -71,16 +97,57 @@
         update = jnp.dot(heads[...], w_o[...], preferred_element_type=F32)
         block = (frames[i].astype(F32) + update).astype(BF16)
         mixed[i] = block
-        hidden_t[i] = normed(block, gain_t[...])
-
-
-def temporal_kernel(columns, allowed, w_qkv, w_o, out, wide, hidden, qkv, heads):
-    total, local_pos, width = columns.shape
+        token = normed(block, gain_t[...]).astype(F32)
+        left = token[:, :half].reshape(devices, tokens // devices, half)
+        right = token[:, half:].reshape(devices, tokens // devices, half)
+        parcels[i] = jnp.concatenate([left, right], axis=1).astype(BF16)
+        pltpu.make_async_copy(parcels.at[i, me], arrived.at[i, me], own_sem.at[i]).start()
+
+        @pl.loop(1, devices)
+        def _(k):
+            peer = lax.rem(me + k, devices)
+            pltpu.make_async_remote_copy(
+                src_ref=parcels.at[i, peer],
+                dst_ref=arrived.at[i, me],
+                send_sem=send_sem.at[i],
+                recv_sem=recv_sem.at[i],
+                device_id=place(peer, groups),
+                device_id_type=MESH_ID,
+            ).start()
+
+    for i in range(count):
+        pltpu.make_async_copy(parcels.at[i, me], arrived.at[i, me], own_sem.at[i]).wait()
+        all_of = pltpu.make_async_remote_copy(
+            src_ref=parcels.at[i, pl.ds(0, devices - 1)],
+            dst_ref=arrived.at[i, pl.ds(0, devices - 1)],
+            send_sem=send_sem.at[i],
+            recv_sem=recv_sem.at[i],
+            device_id=place(lax.rem(me + 1, devices), groups),
+            device_id_type=MESH_ID,
+        )
+        all_of.wait_send()
+        all_of.wait_recv()
+
+
+def temporal_kernel(
+    groups, arrived, allowed, w_all, mixed, out, wide, hidden, qkv, heads, parcels, returned,
+    send_sem, recv_sem, own_sem,
+):
+    count, devices, rows16, half = arrived.shape
+    local_pos, width, total = rows16 // 2, 2 * half, count * devices
+    me = lax.axis_index("dp") * groups + lax.axis_index("grp")
+    barrier = greet_all(me, devices, groups)
     lanes = range(0, width, 128)
-    for g in range(0, total, 16):
-        block = columns[pl.ds(g, 16)].astype(F32).reshape(16 * local_pos, width)
-        for c in lanes:
-            wide[c // 128, pl.ds(g * local_pos, 16 * local_pos), :] = block[:, c : c + 128]
+
+    @pl.loop(0, devices)
+    def _(s):
+        for i in range(count):
+            block = arrived[i, s].astype(F32)
+            rows = pl.ds(pl.multiple_of((s * count + i) * local_pos, local_pos), local_pos)
+            for c in range(0, half, 128):
+                wide[c // 128, rows, :] = block[:local_pos, c : c + 128]
+                wide[(half + c) // 128, rows, :] = block[local_pos:, c : c + 128]
+
     for p in range(local_pos):
         for c in lanes:
             hidden[pl.ds(p * total, total), pl.ds(c, 128)] = wide[
@@ -90,7 +157,7 @@
     @pl.loop(0, 3 * width // 256)
     def _(t):
         cols = pl.ds(pl.multiple_of(t * 256, 256), 256)
-        qkv[:, cols] = jnp.dot(hidden[...], w_qkv[:, cols], preferred_element_type=F32).astype(BF16)
+        qkv[:, cols] = jnp.dot(hidden[...], w_all[:, cols], preferred_element_type=F32).astype(BF16)
 
     mask = jnp.concatenate([allowed[...], allowed[...]], axis=0) > 0.0
     low = lax.broadcasted_iota(jnp.int32, (total, 128), 1) < 64
@@ -108,16 +175,62 @@
             )
 
     for t in range(0, width, 256):
-        update = jnp.dot(heads[...], w_o[:, pl.ds(t, 256)], preferred_element_type=F32)
+        update = jnp.dot(heads[...], w_all[:, pl.ds(3 * width + t, 256)], preferred_element_type=F32)
         for p in range(local_pos):
             for c in range(0, 256, 128):
                 wide[(t + c) // 128, pl.ds(p, total, stride=local_pos), :] = update[
                     p * total : (p + 1) * total, c : c + 128
                 ]
-    for g in range(0, total, 16):
-        for c in lanes:
-            block = wide[c // 128, pl.ds(g * local_pos, 16 * local_pos), :]
-            out[pl.ds(g, 16), :, pl.ds(c, 128)] = block.reshape(16, local_pos, 128).astype(BF16)
+    pl.semaphore_wait(barrier, devices - 1)
+
+    @pl.loop(1, devices + 1)
+    def _(k):
+        peer = lax.rem(me + k, devices)
+        for i in range(count):
+            rows = pl.ds(pl.multiple_of((peer * count + i) * local_pos, local_pos), local_pos)
+            for c in range(0, half, 128):
+                block = jnp.concatenate(
+                    [wide[c // 128, rows, :], wide[(half + c) // 128, rows, :]], axis=0
+                )
+                parcels[peer, pl.ds(i * rows16, rows16), pl.ds(c, 128)] = block.astype(BF16)
+
+        @pl.when(k < devices)
+        def _():
+            pltpu.make_async_remote_copy(
+                src_ref=parcels.at[peer],
+                dst_ref=returned.at[me],
+                send_sem=send_sem,
+                recv_sem=recv_sem,
+                device_id=place(peer, groups),
+                device_id_type=MESH_ID,
+            ).start()
+
+    own = pltpu.make_async_copy(parcels.at[me], returned.at[me], own_sem)
+    own.start()
+    own.wait()
+    all_of = pltpu.make_async_remote_copy(
+        src_ref=parcels.at[pl.ds(0, devices - 1)],
+        dst_ref=returned.at[pl.ds(0, devices - 1)],
+        send_sem=send_sem,
+        recv_sem=recv_sem,
+        device_id=place(lax.rem(me + 1, devices), groups),
+        device_id_type=MESH_ID,
+    )
+    all_of.wait_recv()
+
+    @pl.loop(0, devices // 2)
+    def _(j):
+        for i in range(count):
+            first = returned[2 * j, pl.ds(i * rows16, rows16), :].astype(F32)
+            second = returned[2 * j + 1, pl.ds(i * rows16, rows16), :].astype(F32)
+            rows = pl.ds(pl.multiple_of(j * rows16, rows16), rows16)
+            for h in range(2):
+                part = slice(h * local_pos, (h + 1) * local_pos)
+                update = jnp.concatenate([first[part], second[part]], axis=0)
+                cols = pl.ds(h * half, half)
+                out[i, rows, cols] = (mixed[i, rows, cols].astype(F32) + update).astype(BF16)
+
+    all_of.wait_send()
 
 
 def allowed_frames(episode_len, total):
@@ -130,31 +243,39 @@
 VMEM = pl.BlockSpec(memory_space=pltpu.VMEM)
 
 
-def fused(frames, episode_len, norm_spatial, w_sqkv, w_so, norm_temporal, w_tqkv, w_to):
+def fused(groups, frames, episode_len, norm_spatial, w_sqkv, w_so, norm_temporal, w_tqkv, w_to):
     count, tokens, width = frames.shape
-    full_tqkv = lax.all_gather(w_tqkv, ("dp", "grp"), axis=0, tiled=True)
-    full_to = lax.all_gather(w_to, ("dp", "grp"), axis=0, tiled=True)
-    rows = count * tokens
-    mixed, temporal_in = pl.pallas_call(
-        spatial_kernel,
-        out_shape=[jax.ShapeDtypeStruct(frames.shape, BF16)] * 2,
+    devices = width // w_to.shape[0]
+    w_mine = jnp.concatenate([w_tqkv, w_to], axis=1)
+    w_all = lax.all_gather(w_mine, ("dp", "grp"), axis=0, tiled=True)
+    rows, total, half = count * tokens, count * devices, width // 2
+    block = 2 * tokens // devices
+    mixed, arrived = pl.pallas_call(
+        functools.partial(spatial_kernel, groups),
+        out_shape=[
+            jax.ShapeDtypeStruct(frames.shape, BF16),
+            jax.ShapeDtypeStruct((count, devices, block, half), BF16),
+        ],
         in_specs=[VMEM] * 5,
-        out_specs=[VMEM] * 2,
+        out_specs=[VMEM, pl.BlockSpec(memory_space=pl.ANY)],
         scratch_shapes=[
             pltpu.VMEM((rows, width), BF16),
             pltpu.VMEM((rows, 3 * width), BF16),
             pltpu.VMEM((tokens, width), BF16),
+            pltpu.VMEM((count, devices, block, half), BF16),
+            pltpu.SemaphoreType.DMA((count,)),
+            pltpu.SemaphoreType.DMA((count,)),
+            pltpu.SemaphoreType.DMA((count,)),
         ],
-        compiler_params=pltpu.CompilerParams(vmem_limit_bytes=48 << 20),
+        compiler_params=pltpu.CompilerParams(
+            vmem_limit_bytes=48 << 20, collective_id=0, has_side_effects=True
+        ),
         name="spatial",
     )(frames, norm_spatial.reshape(1, width), w_sqkv, w_so, norm_temporal.reshape(1, width))
-    columns = lax.all_to_all(temporal_in, ("dp", "grp"), split_axis=1, concat_axis=0, tiled=True)
-    total, local_pos, _ = columns.shape
     allowed = allowed_frames(episode_len, total).astype(F32)
-    rows = total * local_pos
-    update = pl.pallas_call(
-        temporal_kernel,
-        out_shape=jax.ShapeDtypeStruct(columns.shape, BF16),
+    return pl.pallas_call(
+        functools.partial(temporal_kernel, groups),
+        out_shape=jax.ShapeDtypeStruct(frames.shape, BF16),
         in_specs=[VMEM] * 4,
         out_specs=VMEM,
         scratch_shapes=[
@@ -162,12 +283,17 @@
             pltpu.VMEM((rows, width), BF16),
             pltpu.VMEM((rows, 3 * width), BF16),
             pltpu.VMEM((rows, width), BF16),
+            pltpu.VMEM((devices, count * block, half), BF16),
+            pltpu.VMEM((devices, count * block, half), BF16),
+            pltpu.SemaphoreType.DMA,
+            pltpu.SemaphoreType.DMA,
+            pltpu.SemaphoreType.DMA,
         ],
-        compiler_params=pltpu.CompilerParams(vmem_limit_bytes=48 << 20),
+        compiler_params=pltpu.CompilerParams(
+            vmem_limit_bytes=48 << 20, collective_id=1, has_side_effects=True
+        ),
         name="temporal",
-    )(columns, allowed, full_tqkv, full_to)
-    returned = lax.all_to_all(update, ("dp", "grp"), split_axis=0, concat_axis=1, tiled=True)
-    return (mixed.astype(F32) + returned.astype(F32)).astype(BF16)
+    )(arrived, allowed, w_all, mixed)
 
 
 def local(frames, episode_len, norm_spatial, w_sqkv, w_so, norm_temporal, w_tqkv, w_to):
@@ -247,7 +373,7 @@
         P(("dp", "grp"), None),
     )
     devices = mesh.shape["dp"] * mesh.shape["grp"]
-    body = fused if devices == 32 else local
+    body = functools.partial(fused, mesh.shape["grp"]) if devices == 32 else local
     return jax.shard_map(
         body, mesh=mesh, in_specs=placed, out_specs=P(("dp", "grp"), None, None), check_vma=False
     )

time: 223 us -> 176 us (0.79); the launches traced: 218 us -> 174 us
  Pallas kernels: 44.1 us -> 126 us
  waiting for transfers between devices: 102 us -> 28.6 us
  blocking collectives: 40.7 us -> 0 us
  starting transfers between devices: 6.24 us -> 0.01 us
  local copies, waits for them, and re-layouts: 9.39 us -> 3.93 us
    pallas_call x2, Pallas kernels: 44.1 us -> 126 us  [the longest x1 63.3 us: fused(): pl.pallas_call(functools.partial(spatial_kernel, groups), out_shape=[jax....]
    all_to_all x1 -> x0, waiting for transfers between devices: 57.1 us -> none  [fused(): lax.all_to_all(temporal_in, ('dp', 'grp'), split_axis=1, concat_axis=0, t...]
    all_to_all x1 -> x0, blocking collectives: 40.7 us -> none  [fused(): lax.all_to_all(update, ('dp', 'grp'), split_axis=0, concat_axis=1, tiled=...]
    all_gather x2 -> x1, waiting for transfers between devices: 43.6 us -> 28.6 us  [fused(): w_all = lax.all_gather(w_mine, ('dp', 'grp'), axis=0, tiled=True)]
    all_to_all x1 -> x0, starting transfers between devices: 6.2 us -> none  [fused(): lax.all_to_all(temporal_in, ('dp', 'grp'), split_axis=1, concat_axis=0, t...]
    pallas_call x1 -> x0, local copies, waits for them, and re-layouts: 2.67 us -> none  [fused(): pl.pallas_call(spatial_kernel, out_shape=[jax.ShapeDtypeStruct(frames.sha...]
    all_to_all x1 -> x0, local copies, waits for them, and re-layouts: 2.35 us -> none  [fused(): lax.all_to_all(temporal_in, ('dp', 'grp'), split_axis=1, concat_axis=0, t...]
  transfers between devices with their start and end apart: 3 -> 1, of which waited for: 2 -> 1; matrix products, arithmetic and copies ran while one was open for 2% -> 1% of each run, Pallas kernels for 10% -> 36%
where the time goes in v2:
time: 176 us; the launch traced here: 174 us
  Pallas kernels  126 us (72%)
  waiting for transfers between devices  28.6 us (16%)
  between operations  13.4 us (8%)
  local copies, waits for them, and re-layouts  3.93 us (2%)
  other arithmetic  2.69 us (2%)
    pallas_call x1, Pallas kernels, fused(): pl.pallas_call(functools.partial(spatial_kernel, groups), out_shape=[jax....  63.3 us
    pallas_call x1, Pallas kernels, fused(): pl.pallas_call(functools.partial(temporal_kernel, groups), out_shape=jax....  62.4 us
    all_gather x1, waiting for transfers between devices, fused(): w_all = lax.all_gather(w_mine, ('dp', 'grp'), axis=0, tiled=True)  28.6 us
    unnamed x7, local copies, waits for them, and re-layouts  3.93 us
  transfers between devices with their start and end apart: 1, of which 1 were waited for; matrix products, arithmetic and copies ran while one was open for 1% of the time, Pallas kernels for 36%

profile of v2, /device:TPU:31, one launch (start us, length us, event | category | flops | bytes accessed | tf_op | source)
XLA Modules:
  0.0 174.3 jit_solution(14583183243122999587)
XLA Ops:
  6.5 0.0 all-gather.2.cloned.1.call-start
  6.5 1.7 pad_maximum_fusion
  8.2 0.0 all-gather.2.cloned.1.call-update
  8.2 0.8 reduce-window.8
  9.1 0.0 copy-start
  9.1 1.4 copy-done
  10.5 0.0 copy-start.1
  10.5 0.7 copy-done.1
  11.2 0.0 copy-start.2
  11.2 0.7 copy-done.2
  11.9 63.3 %spatial.1 = (bf16[3,256,1024]{2,1,0:T(8,128)(2,1)S(1)}, bf16[3,32,16,512]{3,2,1,0:T(8,128)(2,1)S(1)}) custom-call(bf16[3,256,1024]{2,1,0:T(8,128)(2,1)S(1)} %copy-done, f32[1,1024]{1,0:T(1,128)S(1)} %bitcast.4, bf16[1024,3072]{1,0:T(8,128)(2,1)} %w_qkv.1, bf16[1024,1024]{1,0:T(8,128)(2,1)} %w_o.1, f32[1,1024]{1,0:T(1,128)S(1)} %bitcast.5), custom_call_target="tpu_custom_call" | custom-call | tf_op jit(solution)/shard_map/spatial/pallas_call | solution.py:253
  75.2 0.1 convert_reduce_fusion
  75.3 0.1 fusion.1.allowed
  75.4 28.6 %all-gather.2.cloned.1.call-done.w_all = bf16[1024,4096]{1,0:T(8,128)(2,1)} async-done(((bf16[32,4096]{1,0:T(8,128)(2,1)}), bf16[1024,4096]{1,0:T(8,128)(2,1)}) %all-gather.2.cloned.1.call-update) | async-done | bytes 8388624 | tf_op jit(solution)/shard_map/all_gather | solution.py:250
  104.0 62.4 %temporal.1 = bf16[3,256,1024]{2,1,0:T(8,128)(2,1)S(1)} custom-call(bf16[3,32,16,512]{3,2,1,0:T(8,128)(2,1)S(1)} %get-tuple-element.7.arrived, f32[96,96]{1,0:T(8,128)S(1)} %fusion.1.allowed, bf16[1024,4096]{1,0:T(8,128)(2,1)} %all-gather.2.cloned.1.call-done.w_all, bf16[3,256,1024]{2,1,0:T(8,128)(2,1)S(1)} %get-tuple-element.8.mixed), custom_call_target="tpu_custom_call" | custom-call | tf_op jit(solution)/shard_map/temporal/pallas_call | solution.py:276
  166.4 1.1 copy.10
Async XLA Ops:
  6.5 97.4 %all-gather.2.cloned.1.call-start = ((), (), s32[]{:S(2)}) async-start(), calls=%async_computation | async-start | bytes 8650752 | tf_op jit(solution)/shard_map/all_gather | solution.py:250
  9.1 1.4 copy-start
  10.5 0.7 copy-start.1
  11.2 0.7 copy-start.2
Sparse Core Ops, SparseCore 0:
  10.2 93.7 all-gather.1

commit v3 on v2

--- a/solution.py
+++ b/solution.py
@@ -41,6 +41,69 @@
 MESH_ID = pl.DeviceIdType.MESH
 
 
+def relay(groups, me, mine, full, send_sem, recv_sem):
+    z, y, x, core = me // 8, lax.rem(me // 4, 2), lax.rem(me // 2, 2), lax.rem(me, 2)
+
+    def index(z, y, x, core):
+        return ((z * 2 + y) * 2 + x) * 2 + core
+
+    mate, over_y, over_x = index(z, y, x, 1 - core), index(z, 1 - y, x, core), index(z, y, 1 - x, core)
+
+    def send(source, slot, *peers):
+        for peer in peers:
+            pltpu.make_async_remote_copy(
+                src_ref=source,
+                dst_ref=full.at[slot],
+                send_sem=send_sem,
+                recv_sem=recv_sem.at[slot],
+                device_id=place(peer, groups),
+                device_id_type=MESH_ID,
+            ).start()
+
+    def wait(slot):
+        pltpu.make_async_copy(full.at[slot], full.at[slot], recv_sem.at[slot]).wait()
+
+    def forward(slot, *peers):
+        wait(slot)
+        send(full.at[slot], slot, *peers)
+
+    def far(hop):
+        return (z + 1 - 2 * lax.rem(z, 2), lax.rem(z + 2, 4), 3 - z)[hop]
+
+    def first():
+        line = [index(far(hop), y, x, core) for hop in range(3)]
+        send(mine, me, line[0], over_y, over_x, line[1], line[2], mate)
+
+    def along_z(hop):
+        forward(index(far(hop), y, x, core), over_y, over_x, mate)
+
+    def across():
+        for other in range(4):
+            peers = [over_x, mate] if other % 2 == 0 else [mate]
+            forward(index(other, 1 - y, x, core), *peers)
+            peers = [over_y, mate] if other % 2 == 1 else [mate]
+            forward(index(other, y, 1 - x, core), *peers)
+
+    def corner():
+        for other in range(4):
+            forward(index(other, 1 - y, 1 - x, core), mate)
+
+    def finish():
+        for other in range(16):
+            wait(other * 2 + 1 - core)
+        count = full.shape[0] - 1
+        pltpu.make_async_remote_copy(
+            src_ref=full.at[pl.ds(0, count)],
+            dst_ref=full.at[pl.ds(0, count)],
+            send_sem=send_sem,
+            recv_sem=recv_sem.at[0],
+            device_id=place(mate, groups),
+            device_id_type=MESH_ID,
+        ).wait_send()
+
+    return first, along_z, across, corner, finish
+
+
 def place(index, groups):
     return (index // groups, lax.rem(index, groups))
 
@@ -57,13 +120,14 @@
 
 
 def spatial_kernel(
-    groups, frames, gain_s, w_qkv, w_o, gain_t, mixed, arrived, hidden, qkv, heads, parcels,
-    send_sem, recv_sem, own_sem,
+    groups, frames, gain_s, w_qkv, w_o, gain_t, w_mine, mixed, arrived, full, hidden, qkv, heads,
+    parcels, send_sem, recv_sem, own_sem, relay_send, relay_recv, relay_own,
 ):
     count, tokens, width = frames.shape
     devices, half = parcels.shape[1], width // 2
     me = lax.axis_index("dp") * groups + lax.axis_index("grp")
     barrier = greet_all(me, devices, groups)
+    first, along_z, across, corner, finish = relay(groups, me, w_mine, full, relay_send, relay_recv)
     low = lax.broadcasted_iota(jnp.int32, (tokens, 128), 1) < 64
 
     @pl.loop(0, count)
@@ -71,12 +135,17 @@
         rows = pl.ds(pl.multiple_of(i * tokens, tokens), tokens)
         hidden[rows, :] = normed(frames[i], gain_s[...])
 
+    pl.semaphore_wait(barrier, devices - 1)
+    first()
+    own_shard = pltpu.make_async_copy(w_mine, full.at[me], relay_own)
+    own_shard.start()
+
     @pl.loop(0, 3 * width // 256)
     def _(t):
         cols = pl.ds(pl.multiple_of(t * 256, 256), 256)
         qkv[:, cols] = jnp.dot(hidden[...], w_qkv[:, cols], preferred_element_type=F32).astype(BF16)
 
-    pl.semaphore_wait(barrier, devices - 1)
+    along_z(0)
 
     @pl.loop(0, count)
     def _(i):
@@ -115,6 +184,13 @@
                 device_id_type=MESH_ID,
             ).start()
 
+        for hop in (1, 2):
+            pl.when(i == hop - 1)(functools.partial(along_z, hop))
+
+    across()
+    corner()
+    finish()
+    own_shard.wait()
     for i in range(count):
         pltpu.make_async_copy(parcels.at[i, me], arrived.at[i, me], own_sem.at[i]).wait()
         all_of = pltpu.make_async_remote_copy(
@@ -130,13 +206,15 @@
 
 
 def temporal_kernel(
-    groups, arrived, allowed, w_all, mixed, out, wide, hidden, qkv, heads, parcels, returned,
-    send_sem, recv_sem, own_sem,
+    groups, arrived, allowed, w_far, mixed, out, wide, hidden, qkv, heads, parcels, returned, w_all,
+    send_sem, recv_sem, own_sem, load_sem,
 ):
     count, devices, rows16, half = arrived.shape
     local_pos, width, total = rows16 // 2, 2 * half, count * devices
     me = lax.axis_index("dp") * groups + lax.axis_index("grp")
     barrier = greet_all(me, devices, groups)
+    load = pltpu.make_async_copy(w_far, w_all, load_sem)
+    load.start()
     lanes = range(0, width, 128)
 
     @pl.loop(0, devices)
@@ -153,6 +231,8 @@
             hidden[pl.ds(p * total, total), pl.ds(c, 128)] = wide[
                 c // 128, pl.ds(p, total, stride=local_pos), :
             ].astype(BF16)
+
+    load.wait()
 
     @pl.loop(0, 3 * width // 256)
     def _(t):
@@ -241,23 +321,24 @@
 
 
 VMEM = pl.BlockSpec(memory_space=pltpu.VMEM)
+ANY = pl.BlockSpec(memory_space=pl.ANY)
 
 
 def fused(groups, frames, episode_len, norm_spatial, w_sqkv, w_so, norm_temporal, w_tqkv, w_to):
     count, tokens, width = frames.shape
     devices = width // w_to.shape[0]
     w_mine = jnp.concatenate([w_tqkv, w_to], axis=1)
-    w_all = lax.all_gather(w_mine, ("dp", "grp"), axis=0, tiled=True)
     rows, total, half = count * tokens, count * devices, width // 2
     block = 2 * tokens // devices
-    mixed, arrived = pl.pallas_call(
+    mixed, arrived, full = pl.pallas_call(
         functools.partial(spatial_kernel, groups),
         out_shape=[
             jax.ShapeDtypeStruct(frames.shape, BF16),
             jax.ShapeDtypeStruct((count, devices, block, half), BF16),
+            jax.ShapeDtypeStruct((devices,) + w_mine.shape, BF16),
         ],
-        in_specs=[VMEM] * 5,
-        out_specs=[VMEM, pl.BlockSpec(memory_space=pl.ANY)],
+        in_specs=[VMEM] * 5 + [ANY],
+        out_specs=[VMEM, ANY, ANY],
         scratch_shapes=[
             pltpu.VMEM((rows, width), BF16),
             pltpu.VMEM((rows, 3 * width), BF16),
@@ -266,17 +347,20 @@
             pltpu.SemaphoreType.DMA((count,)),
             pltpu.SemaphoreType.DMA((count,)),
             pltpu.SemaphoreType.DMA((count,)),
+            pltpu.SemaphoreType.DMA,
+            pltpu.SemaphoreType.DMA((devices,)),
+            pltpu.SemaphoreType.DMA,
         ],
         compiler_params=pltpu.CompilerParams(
             vmem_limit_bytes=48 << 20, collective_id=0, has_side_effects=True
         ),
         name="spatial",
-    )(frames, norm_spatial.reshape(1, width), w_sqkv, w_so, norm_temporal.reshape(1, width))
+    )(frames, norm_spatial.reshape(1, width), w_sqkv, w_so, norm_temporal.reshape(1, width), w_mine)
     allowed = allowed_frames(episode_len, total).astype(F32)
     return pl.pallas_call(
         functools.partial(temporal_kernel, groups),
         out_shape=jax.ShapeDtypeStruct(frames.shape, BF16),
-        in_specs=[VMEM] * 4,
+        in_specs=[VMEM, VMEM, ANY, VMEM],
         out_specs=VMEM,
         scratch_shapes=[
             pltpu.VMEM((width // 128, rows, 128), F32),
@@ -285,6 +369,8 @@
             pltpu.VMEM((rows, width), BF16),
             pltpu.VMEM((devices, count * block, half), BF16),
             pltpu.VMEM((devices, count * block, half), BF16),
+            pltpu.VMEM((width, 4 * width), BF16),
+            pltpu.SemaphoreType.DMA,
             pltpu.SemaphoreType.DMA,
             pltpu.SemaphoreType.DMA,
             pltpu.SemaphoreType.DMA,
@@ -293,7 +379,7 @@
             vmem_limit_bytes=48 << 20, collective_id=1, has_side_effects=True
         ),
         name="temporal",
-    )(arrived, allowed, w_all, mixed)
+    )(arrived, allowed, full.reshape(width, 4 * width), mixed)
 
 
 def local(frames, episode_len, norm_spatial, w_sqkv, w_so, norm_temporal, w_tqkv, w_to):

time: 176 us -> 138 us (0.78)
  waiting for transfers between devices: 28.6 us -> 0 us
  between operations: 13.4 us -> 0.04 us
  Pallas kernels: 126 us -> 132 us
    all_gather x1 -> x0, waiting for transfers between devices: 28.6 us -> none  [fused(): w_all = lax.all_gather(w_mine, ('dp', 'grp'), axis=0, tiled=True)]
    pallas_call x1, Pallas kernels: 63.3 us -> 67 us  [fused(): pl.pallas_call(functools.partial(spatial_kernel, groups), out_shape=[jax....]
    pallas_call x1, Pallas kernels: 62.4 us -> 64.5 us  [fused(): pl.pallas_call(functools.partial(temporal_kernel, groups), out_shape=jax....]
  transfers between devices with their start and end apart: 1 -> 0, of which waited for: 1 -> 0; matrix products, arithmetic and copies ran while one was open for 1% -> 0% of each run, Pallas kernels for 36% -> 0%
where the time goes in v3:
time: 138 us; the launch traced here: 137 us
  Pallas kernels  132 us (96%)
  local copies, waits for them, and re-layouts  3.92 us (3%)
  other arithmetic  1.99 us (1%)
    pallas_call x1, Pallas kernels, fused(): pl.pallas_call(functools.partial(spatial_kernel, groups), out_shape=[jax....  67 us
    pallas_call x1, Pallas kernels, fused(): pl.pallas_call(functools.partial(temporal_kernel, groups), out_shape=jax....  64.5 us
    unnamed x7, local copies, waits for them, and re-layouts  3.92 us

profile of v3, /device:TPU:31, one launch (start us, length us, event | category | flops | bytes accessed | tf_op | source)
XLA Modules:
  0.0 137.5 jit_solution(13936632814914844280)
XLA Ops:
  0.0 0.8 reduce-window.8
  0.8 0.1 convert_reduce_fusion
  0.9 0.1 fusion.1.allowed
  1.0 1.0 pad_maximum_fusion.w_mine
  2.0 0.0 copy-start
  2.0 1.4 %copy-done = bf16[3,256,1024]{2,1,0:T(8,128)(2,1)S(1)} copy-done((bf16[3,256,1024]{2,1,0:T(8,128)(2,1)S(1)}, bf16[3,256,1024]{2,1,0:T(8,128)(2,1)}, u32[]{:S(2)}) %copy-start) | copy-done | bytes 1572888
  3.4 0.0 copy-start.1
  3.4 0.7 copy-done.1
  4.1 0.0 copy-start.2
  4.1 0.7 copy-done.2
  4.8 67.0 %spatial.1 = (bf16[3,256,1024]{2,1,0:T(8,128)(2,1)S(1)}, bf16[3,32,16,512]{3,2,1,0:T(8,128)(2,1)S(1)}, bf16[32,32,4096]{2,1,0:T(8,128)(2,1)}) custom-call(bf16[3,256,1024]{2,1,0:T(8,128)(2,1)S(1)} %copy-done, f32[1,1024]{1,0:T(1,128)S(1)} %bitcast.5, bf16[1024,3072]{1,0:T(8,128)(2,1)} %w_qkv.1, bf16[1024,1024]{1,0:T(8,128)(2,1)} %w_o.1, ...), custom_call_target="tpu_custom_call" | custom-call | tf_op jit(solution)/shard_map/spatial/pallas_call | solution.py:333
  71.8 64.5 %temporal.1 = bf16[3,256,1024]{2,1,0:T(8,128)(2,1)S(1)} custom-call(bf16[3,32,16,512]{3,2,1,0:T(8,128)(2,1)S(1)} %get-tuple-element.8.arrived, f32[96,96]{1,0:T(8,128)S(1)} %fusion.1.allowed, bf16[1024,4096]{1,0:T(8,128)(2,1)} %bitcast.7, bf16[3,256,1024]{2,1,0:T(8,128)(2,1)S(1)} %get-tuple-element.10.mixed), custom_call_target="tpu_custom_call" | custom-call | tf_op jit(solution)/shard_map/temporal/pallas_call | solution.py:360
  136.4 1.1 copy.10
Async XLA Ops:
  2.0 1.4 %copy-start = (bf16[3,256,1024]{2,1,0:T(8,128)(2,1)S(1)}, bf16[3,256,1024]{2,1,0:T(8,128)(2,1)}, u32[]{:S(2)}) copy-start(bf16[3,256,1024]{2,1,0:T(8,128)(2,1)} %frames.1) | copy-start | bytes 4718596
  3.4 0.7 copy-start.1
  4.1 0.7 copy-start.2

commit v4 on v3

--- a/solution.py
+++ b/solution.py
@@ -120,13 +120,17 @@
 
 
 def spatial_kernel(
-    groups, frames, gain_s, w_qkv, w_o, gain_t, w_mine, mixed, arrived, full, hidden, qkv, heads,
-    parcels, send_sem, recv_sem, own_sem, relay_send, relay_recv, relay_own,
+    groups, frames, gain_s, w_qkv_far, w_o_far, gain_t, w_mine, mixed, arrived, full, hidden, qkv, heads,
+    parcels, w_qkv, w_o, load_sem, send_sem, recv_sem, own_sem, relay_send, relay_recv, relay_own,
 ):
     count, tokens, width = frames.shape
     devices, half = parcels.shape[1], width // 2
     me = lax.axis_index("dp") * groups + lax.axis_index("grp")
     barrier = greet_all(me, devices, groups)
+    load_qkv = pltpu.make_async_copy(w_qkv_far, w_qkv, load_sem.at[0])
+    load_o = pltpu.make_async_copy(w_o_far, w_o, load_sem.at[1])
+    load_qkv.start()
+    load_o.start()
     first, along_z, across, corner, finish = relay(groups, me, w_mine, full, relay_send, relay_recv)
     low = lax.broadcasted_iota(jnp.int32, (tokens, 128), 1) < 64
 
@@ -139,6 +143,7 @@
     first()
     own_shard = pltpu.make_async_copy(w_mine, full.at[me], relay_own)
     own_shard.start()
+    load_qkv.wait()
 
     @pl.loop(0, 3 * width // 256)
     def _(t):
@@ -146,6 +151,7 @@
         qkv[:, cols] = jnp.dot(hidden[...], w_qkv[:, cols], preferred_element_type=F32).astype(BF16)
 
     along_z(0)
+    load_o.wait()
 
     @pl.loop(0, count)
     def _(i):
@@ -221,7 +227,7 @@
     def _(s):
         for i in range(count):
             block = arrived[i, s].astype(F32)
-            rows = pl.ds(pl.multiple_of((s * count + i) * local_pos, local_pos), local_pos)
+            rows = pl.ds(pl.multiple_of((slot_of(s) * count + i) * local_pos, local_pos), local_pos)
             for c in range(0, half, 128):
                 wide[c // 128, rows, :] = block[:local_pos, c : c + 128]
                 wide[(half + c) // 128, rows, :] = block[local_pos:, c : c + 128]
@@ -239,51 +245,59 @@
         cols = pl.ds(pl.multiple_of(t * 256, 256), 256)
         qkv[:, cols] = jnp.dot(hidden[...], w_all[:, cols], preferred_element_type=F32).astype(BF16)
 
-    mask = jnp.concatenate([allowed[...], allowed[...]], axis=0) > 0.0
-    low = lax.broadcasted_iota(jnp.int32, (total, 128), 1) < 64
-
-    @pl.loop(0, local_pos)
-    def _(p):
-        rows = pl.ds(pl.multiple_of(p * total, total), total)
-        for c in range(0, width, 128):
-            heads[rows, pl.ds(c, 128)] = pair_heads(
-                qkv[rows, pl.ds(c, 128)],
-                qkv[rows, pl.ds(c + width, 128)],
-                qkv[rows, pl.ds(c + 2 * width, 128)],
-                mask,
-                low,
+    part = total // 2
+    low = lax.broadcasted_iota(jnp.int32, (part, 128), 1) < 64
+    mine = lax.rem(slot_of(me), devices // 2)
+    for q in range(2):
+        mask = allowed[q * part : (q + 1) * part, :]
+        mask = jnp.concatenate([mask, mask], axis=0) > 0.0
+
+        @pl.loop(0, local_pos)
+        def _(p):
+            rows = pl.ds(pl.multiple_of(p * total, total), total)
+            asked = pl.ds(pl.multiple_of(p * total + q * part, part), part)
+            for c in range(0, width, 128):
+                heads[pl.ds(pl.multiple_of(p * part, part), part), pl.ds(c, 128)] = pair_heads(
+                    qkv[asked, pl.ds(c, 128)],
+                    qkv[rows, pl.ds(c + width, 128)],
+                    qkv[rows, pl.ds(c + 2 * width, 128)],
+                    mask,
+                    low,
+                )
+
+        for t in range(0, width, 256):
+            update = jnp.dot(
+                heads[...], w_all[:, pl.ds(3 * width + t, 256)], preferred_element_type=F32
             )
-
-    for t in range(0, width, 256):
-        update = jnp.dot(heads[...], w_all[:, pl.ds(3 * width + t, 256)], preferred_element_type=F32)
-        for p in range(local_pos):
-            for c in range(0, 256, 128):
-                wide[(t + c) // 128, pl.ds(p, total, stride=local_pos), :] = update[
-                    p * total : (p + 1) * total, c : c + 128
-                ]
-    pl.semaphore_wait(barrier, devices - 1)
-
-    @pl.loop(1, devices + 1)
-    def _(k):
-        peer = lax.rem(me + k, devices)
-        for i in range(count):
-            rows = pl.ds(pl.multiple_of((peer * count + i) * local_pos, local_pos), local_pos)
-            for c in range(0, half, 128):
-                block = jnp.concatenate(
-                    [wide[c // 128, rows, :], wide[(half + c) // 128, rows, :]], axis=0
-                )
-                parcels[peer, pl.ds(i * rows16, rows16), pl.ds(c, 128)] = block.astype(BF16)
-
-        @pl.when(k < devices)
-        def _():
-            pltpu.make_async_remote_copy(
-                src_ref=parcels.at[peer],
-                dst_ref=returned.at[me],
-                send_sem=send_sem,
-                recv_sem=recv_sem,
-                device_id=place(peer, groups),
-                device_id_type=MESH_ID,
-            ).start()
+            for p in range(local_pos):
+                for c in range(0, 256, 128):
+                    wide[
+                        (t + c) // 128, pl.ds(q * part * local_pos + p, part, stride=local_pos), :
+                    ] = update[p * part : (p + 1) * part, c : c + 128]
+        if q == 0:
+            pl.semaphore_wait(barrier, devices - 1)
+
+        @pl.loop(0, devices // 2)
+        def _(k):
+            peer = device_of(lax.rem(mine + k + 1, devices // 2) + q * (devices // 2))
+            for i in range(count):
+                rows = pl.ds(pl.multiple_of((slot_of(peer) * count + i) * local_pos, local_pos), local_pos)
+                for c in range(0, half, 128):
+                    block = jnp.concatenate(
+                        [wide[c // 128, rows, :], wide[(half + c) // 128, rows, :]], axis=0
+                    )
+                    parcels[peer, pl.ds(i * rows16, rows16), pl.ds(c, 128)] = block.astype(BF16)
+
+            @pl.when(peer != me)
+            def _():
+                pltpu.make_async_remote_copy(
+                    src_ref=parcels.at[peer],
+                    dst_ref=returned.at[me],
+                    send_sem=send_sem,
+                    recv_sem=recv_sem,
+                    device_id=place(peer, groups),
+                    device_id_type=MESH_ID,
+                ).start()
 
     own = pltpu.make_async_copy(parcels.at[me], returned.at[me], own_sem)
     own.start()
@@ -313,9 +327,18 @@
     all_of.wait_send()
 
 
-def allowed_frames(episode_len, total):
+def slot_of(device):
+    return lax.rem(device // 4, 2) * 16 + device // 8 * 4 + lax.rem(device, 4)
+
+
+def device_of(slot):
+    return lax.rem(slot, 16) // 4 * 8 + slot // 16 * 4 + lax.rem(slot, 4)
+
+
+def allowed_frames(episode_len, total, count):
     ends = jnp.cumsum(episode_len)
-    position = jnp.arange(total, dtype=jnp.int32)
+    row = jnp.arange(total, dtype=jnp.int32)
+    position = device_of(row // count) * count + lax.rem(row, count)
     episode = jnp.sum((position[:, None] >= ends[None, :]).astype(jnp.int32), axis=1)
     return (position[None, :] <= position[:, None]) & (episode[None, :] == episode[:, None])
 
@@ -337,13 +360,16 @@
             jax.ShapeDtypeStruct((count, devices, block, half), BF16),
             jax.ShapeDtypeStruct((devices,) + w_mine.shape, BF16),
         ],
-        in_specs=[VMEM] * 5 + [ANY],
+        in_specs=[VMEM, VMEM, ANY, ANY, VMEM, ANY],
         out_specs=[VMEM, ANY, ANY],
         scratch_shapes=[
             pltpu.VMEM((rows, width), BF16),
             pltpu.VMEM((rows, 3 * width), BF16),
             pltpu.VMEM((tokens, width), BF16),
             pltpu.VMEM((count, devices, block, half), BF16),
+            pltpu.VMEM(w_sqkv.shape, BF16),
+            pltpu.VMEM(w_so.shape, BF16),
+            pltpu.SemaphoreType.DMA((2,)),
             pltpu.SemaphoreType.DMA((count,)),
             pltpu.SemaphoreType.DMA((count,)),
             pltpu.SemaphoreType.DMA((count,)),
@@ -356,7 +382,7 @@
         ),
         name="spatial",
     )(frames, norm_spatial.reshape(1, width), w_sqkv, w_so, norm_temporal.reshape(1, width), w_mine)
-    allowed = allowed_frames(episode_len, total).astype(F32)
+    allowed = allowed_frames(episode_len, total, count).astype(F32)
     return pl.pallas_call(
         functools.partial(temporal_kernel, groups),
         out_shape=jax.ShapeDtypeStruct(frames.shape, BF16),
@@ -366,7 +392,7 @@
             pltpu.VMEM((width // 128, rows, 128), F32),
             pltpu.VMEM((rows, width), BF16),
             pltpu.VMEM((rows, 3 * width), BF16),
-            pltpu.VMEM((rows, width), BF16),
+            pltpu.VMEM((rows // 2, width), BF16),
             pltpu.VMEM((devices, count * block, half), BF16),
             pltpu.VMEM((devices, count * block, half), BF16),
             pltpu.VMEM((width, 4 * width), BF16),

time: 138 us -> 154 us (1.12)
  Pallas kernels: 132 us -> 148 us
    pallas_call x1, Pallas kernels: 64.5 us -> 83.5 us  [fused(): pl.pallas_call(functools.partial(temporal_kernel, groups), out_shape=jax....]
    pallas_call x1, Pallas kernels: 67 us -> 64.1 us  [fused(): pl.pallas_call(functools.partial(spatial_kernel, groups), out_shape=[jax....]
where the time goes in v4:
time: 154 us
  Pallas kernels  148 us (96%)
  local copies, waits for them, and re-layouts  3.92 us (3%)
  other arithmetic  2.03 us (1%)
    pallas_call x1, Pallas kernels, fused(): pl.pallas_call(functools.partial(temporal_kernel, groups), out_shape=jax....  83.5 us
    pallas_call x1, Pallas kernels, fused(): pl.pallas_call(functools.partial(spatial_kernel, groups), out_shape=[jax....  64.1 us
    unnamed x7, local copies, waits for them, and re-layouts  3.92 us

profile of v4, /device:TPU:31, one launch (start us, length us, event | category | flops | bytes accessed | tf_op | source)
XLA Modules:
  0.0 153.6 jit_solution(8880311331918829988)
XLA Ops:
  0.0 0.8 reduce-window.8
  0.9 0.1 convert_reduce_fusion
  1.0 0.1 and_convert_fusion.allowed
  1.1 1.0 pad_maximum_fusion.w_mine
  2.0 0.0 copy-start
  2.1 1.4 copy-done
  3.5 0.0 copy-start.1
  3.5 0.7 copy-done.1
  4.1 0.0 copy-start.2
  4.1 0.7 copy-done.2
  4.8 64.1 %spatial.1 = (bf16[3,256,1024]{2,1,0:T(8,128)(2,1)S(1)}, bf16[3,32,16,512]{3,2,1,0:T(8,128)(2,1)S(1)}, bf16[32,32,4096]{2,1,0:T(8,128)(2,1)}) custom-call(bf16[3,256,1024]{2,1,0:T(8,128)(2,1)S(1)} %copy-done, f32[1,1024]{1,0:T(1,128)S(1)} %bitcast.5, bf16[1024,3072]{1,0:T(8,128)(2,1)} %w_qkv_far.1, bf16[1024,1024]{1,0:T(8,128)(2,1)} %w_o_far.1, ...), custom_call_target="tpu_custom_call" | custom-call | tf_op jit(solution)/shard_map/spatial/pallas_call | solution.py:356
  68.9 83.5 %temporal.1 = bf16[3,256,1024]{2,1,0:T(8,128)(2,1)S(1)} custom-call(bf16[3,32,16,512]{3,2,1,0:T(8,128)(2,1)S(1)} %get-tuple-element.8.arrived, f32[96,96]{1,0:T(8,128)S(1)} %and_convert_fusion.allowed, bf16[1024,4096]{1,0:T(8,128)(2,1)} %bitcast.7, bf16[3,256,1024]{2,1,0:T(8,128)(2,1)S(1)} %get-tuple-element.10.mixed), custom_call_target="tpu_custom_call" | custom-call | tf_op jit(solution)/shard_map/temporal/pallas_call | solution.py:386
  152.4 1.1 copy.10
  (1 shorter events, 0.0 us)
Async XLA Ops:
  2.0 1.4 copy-start
  3.5 0.7 copy-start.1
  4.1 0.7 copy-start.2

commit v5 on v4

--- a/solution.py
+++ b/solution.py
@@ -328,11 +328,11 @@
 
 
 def slot_of(device):
-    return lax.rem(device // 4, 2) * 16 + device // 8 * 4 + lax.rem(device, 4)
+    return lax.rem(device, 2) * 16 + device // 2
 
 
 def device_of(slot):
-    return lax.rem(slot, 16) // 4 * 8 + slot // 16 * 4 + lax.rem(slot, 4)
+    return lax.rem(slot, 16) * 2 + slot // 16
 
 
 def allowed_frames(episode_len, total, count):

time: 154 us -> 150 us (0.974)
  Pallas kernels: 148 us -> 144 us
    pallas_call x1, Pallas kernels: 83.5 us -> 79.7 us  [fused(): pl.pallas_call(functools.partial(temporal_kernel, groups), out_shape=jax....]
where the time goes in v5:
time: 150 us
  Pallas kernels  144 us (96%)
  local copies, waits for them, and re-layouts  3.92 us (3%)
  other arithmetic  2.02 us (1%)
    pallas_call x1, Pallas kernels, fused(): pl.pallas_call(functools.partial(temporal_kernel, groups), out_shape=jax....  79.7 us
    pallas_call x1, Pallas kernels, fused(): pl.pallas_call(functools.partial(spatial_kernel, groups), out_shape=[jax....  64.1 us
    unnamed x7, local copies, waits for them, and re-layouts  3.92 us

profile of v5, /device:TPU:31, one launch (start us, length us, event | category | flops | bytes accessed | tf_op | source)
XLA Modules:
  0.0 149.7 jit_solution(9384840858251189506)
XLA Ops:
  0.0 0.8 reduce-window.8
  0.9 0.1 convert_reduce_fusion
  0.9 0.1 and_convert_fusion.allowed
  1.0 1.0 pad_maximum_fusion.w_mine
  2.0 0.0 copy-start
  2.0 1.4 copy-done
  3.4 0.0 copy-start.1
  3.4 0.7 copy-done.1
  4.1 0.0 copy-start.2
  4.1 0.7 copy-done.2
  4.8 64.1 %spatial.1 = (bf16[3,256,1024]{2,1,0:T(8,128)(2,1)S(1)}, bf16[3,32,16,512]{3,2,1,0:T(8,128)(2,1)S(1)}, bf16[32,32,4096]{2,1,0:T(8,128)(2,1)}) custom-call(bf16[3,256,1024]{2,1,0:T(8,128)(2,1)S(1)} %copy-done, f32[1,1024]{1,0:T(1,128)S(1)} %bitcast.5, bf16[1024,3072]{1,0:T(8,128)(2,1)} %w_qkv_far.1, bf16[1024,1024]{1,0:T(8,128)(2,1)} %w_o_far.1, ...), custom_call_target="tpu_custom_call" | custom-call | tf_op jit(solution)/shard_map/spatial/pallas_call | solution.py:356
  68.9 79.7 %temporal.1 = bf16[3,256,1024]{2,1,0:T(8,128)(2,1)S(1)} custom-call(bf16[3,32,16,512]{3,2,1,0:T(8,128)(2,1)S(1)} %get-tuple-element.8.arrived, f32[96,96]{1,0:T(8,128)S(1)} %and_convert_fusion.allowed, bf16[1024,4096]{1,0:T(8,128)(2,1)} %bitcast.7, bf16[3,256,1024]{2,1,0:T(8,128)(2,1)S(1)} %get-tuple-element.10.mixed), custom_call_target="tpu_custom_call" | custom-call | tf_op jit(solution)/shard_map/temporal/pallas_call | solution.py:386
  148.6 1.1 copy.10
  (1 shorter events, 0.0 us)
Async XLA Ops:
  2.0 1.4 copy-start
  3.4 0.7 copy-start.1
  4.1 0.7 copy-start.2
